TPU v7x, 32 devices: a whole 2x2x4 slice. The times are simulated.
32 devices in a mesh: row: 4 (over y, core), col: 8 (over z, x).
Axes of the slice: x: 2, y: 2, z: 4, core: 2. Of those that a mesh axis runs over, the one named last changes fastest.
Arguments:
- tangent: bfloat16 [4, 8, 64, 4096], P('row', 'col')
- block_row: int32 [4, 8, 64], P('row', 'col'), may hold values from 0 to 15
- block_col: int32 [4, 8, 64], P('row', 'col'), may hold values from 0 to 7
- tile_count: int32 [4, 8], P('row', 'col'), may hold values from 1 to 64, 320 in all within a row
- old_basis: bfloat16 [64, 3072], P(('row', 'col'))
- old_id: int32 [64], P(('row', 'col')), may hold values from 0 to 63, as said below
- residual: float32 [4096], P(('row', 'col'))
Outputs:
- recycled_c: bfloat16 [64, 3072], P(('row', 'col'))
- recycled_u: bfloat16 [64, 3072], P(('row', 'col'))
- coefficients: float32 [48], replicated
Inputs may be any that keep to these rules, and one draw needn't show every extreme that they name: old_id is a permutation of the block rows. Write slot s = (16 * r + 2 * c + i) with 0 <= c < 8 and 0 <= i < 2, and p = i // 2. Its new block row is 16 * r + 2 * ((c + p + 1) mod (8)) + 2 * p + e, with e 0 or 1, the two slots of a pair taking different e. In each row of tile_count the largest count is exactly 64.
All inputs are finite; a program needn't handle non-finite values. No bound on the sum of `tile_count` on one device may be relied on, other than what follows from the above.
Results may differ from a plain program's by a relative error of at most 0.0012.
Values may be sent and summed in bfloat16 or wider, within the bound.
A program may use at most 64 MiB of HBM per device.

v0:
```python
import math

import jax
import jax.numpy as jnp
from jax import lax
from jax.sharding import PartitionSpec as P

BLK = 64
K = 48


def passed_along(array, axis, by):
    peers = lax.axis_size(axis)
    return lax.ppermute(array, axis, [(i, (i + by) % peers) for i in range(peers)])


def per_device(tangent, block_row, block_col, tile_count, old_basis, old_id, residual):
    highest = lax.Precision.HIGHEST
    per_dev = old_basis.shape[0]
    col_count = lax.axis_size("col")
    row_count = lax.axis_size("row")
    new_slot = old_id % per_dev
    labels = (new_slot - 0 + 1).astype(jnp.bfloat16)
    incoming, in_labels = passed_along((old_basis, labels), "col", 1)
    wanted = jnp.arange(1, 3, dtype=jnp.float32)
    placing = (in_labels.astype(jnp.float32)[None, :] == wanted[:, None]).astype(jnp.bfloat16)
    placed = jnp.dot(placing, incoming, preferred_element_type=jnp.float32).astype(jnp.bfloat16)
    col_basis = lax.all_gather(placed, "row", axis=0, tiled=True)
    values = tangent[0, 0]
    rows_local = block_row[0, 0]
    cols_local = block_col[0, 0]
    live_count = tile_count[0, 0]
    stored = values.shape[0]
    group = min(128, stored)
    tile_rows = per_dev * col_count

    def add_group(index, partial_value):
        start = index * group
        block_vals = values.reshape(group, BLK, BLK)
        picked = col_basis[cols_local].reshape(group, BLK, K)
        prods = jnp.einsum("gij,gjk->gik", block_vals, picked, preferred_element_type=jnp.float32)
        alive = start + jnp.arange(group, dtype=jnp.int32) < live_count
        prods = jnp.where(alive[:, None, None], prods, jnp.float32(0.0)).reshape(group, BLK * K)
        return partial_value.at[rows_local].add(prods)

    trips = (live_count + group - 1) // group
    partial_value = lax.fori_loop(0, trips, add_group, jnp.zeros((tile_rows, BLK * K), jnp.float32))
    product = lax.psum_scatter(partial_value, "col", scatter_dimension=0, tiled=True)
    flat_c = product.reshape(per_dev * BLK, K)
    total_rows = per_dev * row_count * col_count * BLK
    gram_part = jnp.dot(flat_c.T, flat_c, precision=highest)
    gram = lax.psum(gram_part, ("row", "col"))
    lower = jnp.linalg.cholesky(gram / jnp.float32(total_rows))
    ortho_t = jax.scipy.linalg.solve_triangular(lower, flat_c.T, lower=True)
    inner = lax.psum(jnp.dot(ortho_t, residual, precision=highest), ("row", "col"))
    coefficients = inner / jnp.float32(math.sqrt(total_rows))
    basis_t = jax.scipy.linalg.solve_triangular(
        lower, placed.astype(jnp.float32).reshape(per_dev * BLK, K).T, lower=True
    )
    recycled_c = ortho_t.T.reshape(per_dev, BLK * K).astype(jnp.bfloat16)
    recycled_u = basis_t.T.reshape(per_dev, BLK * K).astype(jnp.bfloat16)
    return (recycled_c, recycled_u, coefficients)


def solution(mesh):
    return jax.shard_map(
        per_device,
        mesh=mesh,
        in_specs=(
            P("row", "col", None, None),
            P("row", "col", None),
            P("row", "col", None),
            P("row", "col"),
            P(("row", "col"), None),
            P(("row", "col")),
            P(("row", "col")),
        ),
        out_specs=(P(("row", "col"), None), P(("row", "col"), None), P()),
        check_vma=False,
    )
```

profile of v0, /device:TPU:0, one launch (start us, length us, event | category | flops | bytes accessed | tf_op | source)
XLA Modules:
  0.0 203.7 jit_solution(17095770155773927274)
XLA Ops:
  7.2 3.0 %collective-permute-start.1 = (bf16[2,3072]{1,0:T(2,128)(2,1)}, bf16[2,3072]{1,0:T(2,128)(2,1)S(1)}, u32[]{:S(2)}, u32[]{:S(2)}) collective-permute-start(bf16[2,3072]{1,0:T(2,128)(2,1)} %param.15), channel_id=1, source_target_pairs={{0,1},{1,2},{2,3},{3,4},{4,5},{5,6},{6,7},{7,0},{8,9},{9,10},{10,1... | collective-permute-start | bytes 36872 | tf_op jit(solution)/shard_map/ppermute | solution.py:14
  10.2 0.7 fusion.12
  10.9 1.5 collective-permute-start
  13.1 4.0 %collective-permute-done = bf16[2]{0:T(256)(128)(2,1)S(1)} collective-permute-done((bf16[2]{0:T(256)(128)(2,1)S(1)}, bf16[2]{0:T(256)(128)(2,1)S(1)}, u32[]{:S(2)}, u32[]{:S(2)}) %collective-permute-start) | collective-permute-done | bytes 36 | tf_op jit(solution)/shard_map/ppermute | solution.py:14
  17.3 5.2 %all-gather = bf16[4,2,3072]{2,1,0:T(2,128)(2,1)S(1)} all-gather(bf16[1,2,3072]{2,1,0:T(2,128)(2,1)S(1)} %bitcast.62), channel_id=1, replica_groups=mesh['row'=4,'col'=8] {'row'}, dimensions={0}, use_global_device_ids=true | all-gather | bytes 61440 | tf_op jit(solution)/shard_map/all_gather | solution.py:28
  22.6 11.6 %while.10 = (s32[]{:T(128)}, f32[16,3072]{1,0:T(8,128)S(1)}, s32[]{:T(128)}, s32[64]{0:T(128)}, s32[]{:T(128)}, /*index=5*/s32[64]{0:T(128)}, bf16[8,3072]{1,0:T...) while((s32[]{:T(128)}, f32[16,3072]{1,0:T(8,128)S(1)}, s32[]{:T(128)}, s32[64]{0:T(128)}, ...), condition=%wide.region_2.3_spmd, body=%wide.region_0.2_spmd.sunk | while | flops 25560580 | bytes 11933725 | solution.py:47
  22.6 0.7 fusion.29
  23.3 0.8 gather_fusion
  24.1 1.1 reshape.106
  25.2 1.1 reshape_squeeze.4
  26.3 0.7 add_compare_fusion.2
  27.0 1.9 select_bitcast_fusion.2
  28.9 1.9 copy.28
  30.8 1.8 reshape.107
  32.5 1.7 scatter_fusion
  34.3 0.7 copy-done.1
  36.3 67.4 %all-reduce.3.cloned.1.call-done = f32[16,3072]{1,0:T(8,128)} async-done(((f32[16,3072]{1,0:T(8,128)}), f32[16,3072]{1,0:T(8,128)}) %all-reduce.3.cloned.1.call-update) | async-done | bytes 196624
  103.7 0.9 constant_dynamic-slice_fusion
  105.0 39.6 %psum.14 = f32[48,48]{0,1:T(8,128)S(1)} all-reduce(f32[48,48]{0,1:T(8,128)S(1)} %fusion.17), channel_id=1, replica_groups=mesh['row'=4,'col'=8] {'row','col'}, use_global_device_ids=true, to_apply=%region_4.5 | all-reduce | flops 2304 | bytes 18432 | tf_op jit(solution)/shard_map/psum | solution.py:52
  144.7 4.4 %cholesky.18 = f32[48,48]{1,0:T(8,128)S(1)} custom-call(f32[48,48]{1,0:T(8,128)S(1)} %fusion.9), custom_call_target="Cholesky" | custom-call | tf_op jit(solution)/shard_map/jit(cholesky)/cholesky | solution.py:53
  150.4 3.7 %custom-call.7 = f32[1,48,48]{1,2,0:T(8,128)S(1)} custom-call(f32[1,48,48]{2,1,0:T(8,128)S(1)} %fusion.6), custom_call_target="InvertDiagBlocksLowerTriangular" | custom-call | tf_op jit(solution)/shard_map/jit(_solve_triangular)/triangular_solve | solution.py:54
  154.5 0.7 convert_element_type.34
  155.6 0.7 convert_element_type.37
  156.5 39.9 %psum.15 = f32[48]{0:T(128)S(1)} all-reduce(f32[48]{0:T(128)S(1)} %convolution_bitcast_fusion), channel_id=1, replica_groups=mesh['row'=4,'col'=8] {'row','col'}, use_global_device_ids=true, to_apply=%region_7.9 | all-reduce | flops 48 | bytes 384 | tf_op jit(solution)/shard_map/psum | solution.py:55
  (33 shorter events, 4.2 us)
Async XLA Ops:
  7.2 149.2 %copy-start = (f32[128]{0:T(128)S(1)}, f32[128]{0:T(128)}, u32[]{:S(2)}) copy-start(f32[128]{0:T(128)} %param.17) | copy-start | bytes 1540
  7.2 96.5 %all-reduce.3.cloned.1.call-start = ((), (), s32[]{:S(2)}) async-start(), calls=%async_computation | async-start | bytes 393216
  7.2 9.9 %collective-permute-start.1 = (bf16[2,3072]{1,0:T(2,128)(2,1)}, bf16[2,3072]{1,0:T(2,128)(2,1)S(1)}, u32[]{:S(2)}, u32[]{:S(2)}) collective-permute-start(bf16[2,3072]{1,0:T(2,128)(2,1)} %param.15), channel_id=1, source_target_pairs={{0,1},{1,2},{2,3},{3,4},{4,5},{5,6},{6,7},{7,0},{8,9},{9,10},{10,1... | collective-permute-start | bytes 36872 | tf_op jit(solution)/shard_map/ppermute | solution.py:14
  10.9 6.2 %collective-permute-start = (bf16[2]{0:T(256)(128)(2,1)S(1)}, bf16[2]{0:T(256)(128)(2,1)S(1)}, u32[]{:S(2)}, u32[]{:S(2)}) collective-permute-start(bf16[2]{0:T(256)(128)(2,1)S(1)} %fusion.12), channel_id=1, source_target_pairs={{0,1},{1,2},{2,3},{3,4},{4,5},{5,6},{6,7},{7,0},{8,9},{9,10},{10,1... | collective-permute-start | bytes 20 | tf_op jit(solution)/shard_map/ppermute | solution.py:14
  22.6 12.4 %copy-start.3 = (u32[32]{0:T(128)S(1)}, u32[32]{0:T(128)}, u32[]{:S(2)}) copy-start(u32[32]{0:T(128)} %constant.105) | copy-start | bytes 388
  24.1 1.1 copy-start.2
  34.2 0.7 copy-start.1
Sparse Core Ops, SparseCore 0:
  35.1 68.5 all-reduce.2
where the time goes:
time: 204 us
  blocking collectives  84.7 us (42%)
  waiting for transfers between devices  71.4 us (35%)
  between operations  15.5 us (8%)
  other arithmetic  13.6 us (7%)
  local copies, waits for them, and re-layouts  10.8 us (5%)
  starting transfers between devices  4.58 us (2%)
  matrix products  3.01 us (1%)
    unnamed x2, waiting for transfers between devices  67.4 us
    psum x1, blocking collectives, per_device(): lax.psum(jnp.dot(ortho_t, residual, precision=highest), ('row', 'col'))  39.9 us
    psum x1, blocking collectives, per_device(): gram = lax.psum(gram_part, ('row', 'col'))  39.6 us
    all_gather x1, blocking collectives, per_device(): col_basis = lax.all_gather(placed, 'row', axis=0, tiled=True)  5.23 us
    another operation x3, other arithmetic, per_device(): lower = jnp.linalg.cholesky(gram / jnp.float32(total_rows))  5.05 us
    ppermute x2, starting transfers between devices, passed_along(): lax.ppermute(array, axis, [(i, (i + by) % peers) for i in range(peers)])  4.54 us
    another operation x2, other arithmetic, per_device(): ortho_t = jax.scipy.linalg.solve_triangular(lower, flat_c.T, lower=True)  4.32 us
  transfers between devices with their start and end apart: 3, of which 2 were waited for; matrix products, arithmetic and copies ran while one was open for 1% of the time, Pallas kernels for 0%

commit v1 on v0

v1 whole, which is shorter than its diff:
```python
import functools
import math

import jax
import jax.numpy as jnp
from jax import lax
from jax.experimental import pallas as pl
from jax.experimental.pallas import tpu as pltpu
from jax.sharding import PartitionSpec as P

BLK = 64
K = 48
OCT = BLK // 8
WIDE = 8 * K
SIDE = 64
MESH = pl.DeviceIdType.MESH
F32 = jnp.float32
BF16 = jnp.bfloat16


def iota(shape, dim):
    return lax.broadcasted_iota(jnp.int32, shape, dim)


def over_k(index, most):
    whole = jnp.zeros_like(index)
    for step in range(1, most):
        whole += (index >= K * step).astype(jnp.int32)
    return whole


def pieces(x):
    hi = x.astype(BF16)
    rest = x - hi.astype(F32)
    mid = rest.astype(BF16)
    lo = (rest - mid.astype(F32)).astype(BF16)
    return hi, mid, lo


def kernel(n_row, n_col, tile_rows, tile_cols, tan_hbm, rows_ref, cols_ref, count_ref, basis_ref, id_ref, res_ref,
           c_ref, u_ref, coef_ref,
           tan, xs, xr, w, a, ps, pr, ga, gb,
           tan_sem, bs_send, bs_recv, p_send, p_recv, ga_send, ga_recv, gb_send, gb_recv):
    r = lax.axis_index("row")
    c = lax.axis_index("col")
    nxt = lax.rem(c + 1, n_col)
    prv = lax.rem(c + n_col - 1, n_col)
    small = tile_cols <= 8
    total = n_row * n_col * 2 * BLK

    load = pltpu.make_async_copy(tan_hbm.at[0, 0], tan, tan_sem)
    load.start()

    barrier = pltpu.get_barrier_semaphore()
    greeted = 0
    for d in range(1, n_row):
        other = lax.rem(r + d, n_row)
        for to in (c, nxt, prv):
            pl.semaphore_signal(barrier, inc=1, device_id=(other, to), device_id_type=MESH)
            greeted += 1
    for d in range(1, n_col):
        pl.semaphore_signal(barrier, inc=1, device_id=(r, lax.rem(c + d, n_col)), device_id_type=MESH)
        greeted += 1

    flat = basis_ref[...].astype(F32)
    held = [jnp.concatenate([flat[s:s + 1, WIDE * g:WIDE * (g + 1)] for g in range(OCT)], axis=0) for s in range(2)]
    swapped = jnp.full((OCT, WIDE), id_ref[0] & 1, jnp.int32) == 1
    xs[...] = jnp.concatenate(
        [jnp.where(swapped, held[1], held[0]), jnp.where(swapped, held[0], held[1])], axis=0
    ).astype(BF16)

    pl.semaphore_wait(barrier, greeted)
    basis_out = []
    for d in range(n_row):
        to = lax.rem(r + d, n_row)
        copy = pltpu.make_async_remote_copy(
            src_ref=xs, dst_ref=xr.at[r], send_sem=bs_send.at[d], recv_sem=bs_recv.at[r],
            device_id=(to, nxt), device_id_type=MESH)
        copy.start()
        basis_out.append(copy)

    load.wait()
    stored = tan.shape[0]
    place = cols_ref[...] * tile_rows + rows_ref[...]
    place = jnp.where(iota((1, stored), 1) < count_ref[...], place, -1)

    def dense(first, many, g):
        hot = (iota((many, stored), 0) + first == place).astype(F32).astype(BF16)
        d = jnp.dot(hot, tan[:, 512 * g:512 * (g + 1)], preferred_element_type=F32)
        hi = d.astype(BF16)
        return hi, (d - hi.astype(F32)).astype(BF16)

    if small:
        for g in range(OCT):
            both = dense(0, tile_cols * tile_rows, g)
            for part in range(2):
                for h in range(2):
                    at = ((part * 2 + h) * OCT + g) * tile_rows
                    for j in range(tile_cols):
                        a[at:at + tile_rows, 256 * j:256 * (j + 1)] = (
                            both[part][tile_rows * j:tile_rows * (j + 1), 256 * h:256 * (h + 1)])

    lane_k = over_k(iota((8, WIDE), 1), 8)
    own_lane = lane_k == iota((8, WIDE), 0)
    spread_row = iota((WIDE, 256), 0)
    spread_col = iota((WIDE, 256), 1)
    spread = jnp.logical_and(
        spread_row - K * over_k(spread_row, 8) == spread_col - K * over_k(spread_col, 4),
        spread_col < 4 * K).astype(F32).astype(BF16)
    quarter = over_k(iota((BLK, 256), 1), 5)

    own = iota((128, 128), 0)
    wanted = (own & 15) * 8 + lax.shift_right_logical(own, 4)
    res_rows = jnp.where(iota((128, 128), 1) == wanted, jnp.broadcast_to(res_ref[...], (128, 128)), 0.0)
    at_k = (iota((128, 128), 1) == K).astype(F32).astype(BF16)
    res_col = jnp.zeros((128, 128), F32)
    for piece in reversed(pieces(res_rows)):
        res_col += jnp.dot(piece, at_k, preferred_element_type=F32)
    tile_row = iota((128, WIDE), 0)
    tile_col = iota((128, WIDE), 1)
    tile = (tile_row - SIDE == tile_col - K * over_k(tile_col, 8)).astype(F32).astype(BF16)

    for q in range(n_row):
        pltpu.make_async_remote_copy(
            src_ref=xs, dst_ref=xr.at[q], send_sem=bs_send.at[0], recv_sem=bs_recv.at[q],
            device_id=(r, nxt), device_id_type=MESH).wait_recv()

    for q in range(n_row):
        blocks = xr[q].astype(F32)
        opened = jnp.concatenate(
            [jnp.where(own_lane, jnp.broadcast_to(blocks[s:s + 1], (8, WIDE)), 0.0) for s in range(2 * OCT)],
            axis=0).astype(BF16)
        wide = jnp.dot(opened, spread, preferred_element_type=F32)
        for m in range(2):
            for e in range(4):
                at = (2 * q + m) * 256 + e * BLK
                w[at:at + BLK, :] = jnp.where(quarter == e, wide[BLK * m:BLK * (m + 1)], 0.0).astype(BF16)

    def put(g, left, right):
        turned = pltpu.roll(right, 64, 1)
        row = pl.ds(g, tile_rows, stride=OCT)
        ps[0, row, :] = left[:, 0:128]
        ps[1, row, :] = left[:, 128:256] + turned[:, 0:128]
        ps[2, row, :] = turned[:, 128:256]

    half = OCT * tile_rows
    if small:
        prod = jnp.dot(a[...], w[...], preferred_element_type=F32)
        prod = prod[:2 * half] + prod[2 * half:]
        for g in range(OCT):
            put(g, prod[tile_rows * g:tile_rows * (g + 1)], prod[half + tile_rows * g:half + tile_rows * (g + 1)])
    else:
        for g in range(OCT):
            def add(j, acc, g=g):
                hi, lo = dense(j * tile_rows, tile_rows, g)
                lhs = jnp.concatenate([hi[:, :256], hi[:, 256:], lo[:, :256], lo[:, 256:]], axis=0)
                return acc + jnp.dot(lhs, w[pl.ds(pl.multiple_of(j * 256, 256), 256), :], preferred_element_type=F32)
            acc = lax.fori_loop(0, tile_cols, add, jnp.zeros((4 * tile_rows, 256), F32))
            acc = acc[:2 * tile_rows] + acc[2 * tile_rows:]
            put(g, acc[:tile_rows], acc[tile_rows:])

    mine = 2 * OCT
    prod_out = []
    for d in range(1, n_col):
        to = lax.rem(c + d, n_col)
        copy = pltpu.make_async_remote_copy(
            src_ref=ps.at[:, pl.ds(pl.multiple_of(to * mine, mine), mine)], dst_ref=pr.at[c],
            send_sem=p_send.at[d], recv_sem=p_recv.at[c], device_id=(r, to), device_id_type=MESH)
        copy.start()
        prod_out.append(copy)
    product = ps[:, pl.ds(pl.multiple_of(c * mine, mine), mine), :]
    for d in range(1, n_col):
        source = lax.rem(c + d, n_col)
        pltpu.make_async_remote_copy(
            src_ref=ps.at[:, pl.ds(0, mine)], dst_ref=pr.at[source], send_sem=p_send.at[d], recv_sem=p_recv.at[source],
            device_id=(r, source), device_id_type=MESH).wait_recv()
        product += pr[source]
    product = jnp.concatenate([product[0], product[1], product[2]], axis=1)

    lane = iota((2 * OCT, 128), 1)
    turned = [product if b == 0 else pltpu.roll(product, WIDE - K * b, 1) for b in range(8)]
    stacked = jnp.concatenate([jnp.where(lane < K, t[:, :128], 0.0) for t in turned], axis=0) + res_col
    gram = lax.dot_general(stacked, stacked, (((0,), (0,)), ((), ())), precision=lax.Precision.HIGHEST,
                           preferred_element_type=F32)
    packed = gram[:24] + pltpu.roll(gram[24:48], SIDE, 1)

    ga[r] = packed
    sent = []
    for d in range(1, n_row):
        to = lax.rem(r + d, n_row)
        copy = pltpu.make_async_remote_copy(
            src_ref=ga.at[r], dst_ref=ga.at[r], send_sem=ga_send.at[d], recv_sem=ga_recv.at[r],
            device_id=(to, c), device_id_type=MESH)
        copy.start()
        sent.append(copy)
    for d in range(1, n_row):
        source = lax.rem(r + d, n_row)
        pltpu.make_async_remote_copy(
            src_ref=ga.at[r], dst_ref=ga.at[source], send_sem=ga_send.at[d], recv_sem=ga_recv.at[source],
            device_id=(source, c), device_id_type=MESH).wait_recv()
    packed = ga[0]
    for q in range(1, n_row):
        packed += ga[q]
    gb[c] = packed
    for d in range(1, n_col):
        to = lax.rem(c + d, n_col)
        copy = pltpu.make_async_remote_copy(
            src_ref=gb.at[c], dst_ref=gb.at[c], send_sem=gb_send.at[d], recv_sem=gb_recv.at[c],
            device_id=(r, to), device_id_type=MESH)
        copy.start()
        sent.append(copy)
    for d in range(1, n_col):
        source = lax.rem(c + d, n_col)
        pltpu.make_async_remote_copy(
            src_ref=gb.at[c], dst_ref=gb.at[source], send_sem=gb_send.at[d], recv_sem=gb_recv.at[source],
            device_id=(r, source), device_id_type=MESH).wait_recv()
    packed = gb[0]
    for q in range(1, n_col):
        packed += gb[q]

    row_id = iota((K, 128), 0)
    lane_id = iota((K, 128), 1)
    packed = packed * F32(1.0 / total)
    m = jnp.concatenate([packed, pltpu.roll(packed, SIDE, 1)], axis=0)
    m = jnp.where(lane_id < SIDE, m, (lane_id - SIDE == row_id).astype(F32))
    tiles = [m[8 * t:8 * (t + 1)] for t in range(K // 8)]
    sub = iota((8, 128), 0)
    for j in range(K):
        t0, s0 = j // 8, j % 8
        row = jnp.broadcast_to(tiles[t0][s0:s0 + 1, :], (8, 128))
        inv = 1.0 / jnp.broadcast_to(tiles[t0][s0:s0 + 1, j:j + 1], (8, 128))
        scaled = row * inv
        for t in range(t0, K // 8):
            if t == t0 and s0 == 7:
                continue
            col = jnp.broadcast_to(tiles[t][:, j:j + 1], (8, 128))
            if t == t0:
                col = jnp.where(sub > s0, col, 0.0)
            tiles[t] = tiles[t] - col * scaled
    m = jnp.concatenate(tiles, axis=0)
    pivots = jnp.sum(jnp.where(lane_id == row_id, m, 0.0), axis=1, keepdims=True)
    m = m * lax.rsqrt(jnp.broadcast_to(pivots, (K, 128)))
    coef = jnp.broadcast_to(m[:, K:K + 1], (K, 128)) * F32(math.sqrt(total))
    coef_ref[...] = jnp.sum(jnp.where(lane_id == row_id, coef, 0.0), axis=0, keepdims=True)

    inverse = jnp.where(lane_id >= SIDE, m, 0.0)
    diag_row = over_k(iota((K, WIDE), 1), 8)
    left = jnp.concatenate(list(pieces(product)) + [xr[r]], axis=0)
    acc = [None, None]
    for n, piece in enumerate(pieces(inverse)):
        wide = jnp.dot(piece, tile, preferred_element_type=F32)
        big = jnp.concatenate([jnp.where(diag_row == b, wide, 0.0) for b in range(8)], axis=0).astype(BF16)
        out = lax.dot_general(left, big, (((1,), (1,)), ((), ())), preferred_element_type=F32)
        c_part = out[0:mine]
        for extra in range(1, 3 - n):
            c_part = c_part + out[extra * mine:(extra + 1) * mine]
        u_part = out[3 * mine:4 * mine]
        acc = [c_part, u_part] if n == 0 else [acc[0] + c_part, acc[1] + u_part]
    c_ref[...] = acc[0].astype(BF16)
    u_ref[...] = acc[1].astype(BF16)

    for copy in basis_out + prod_out + sent:
        copy.wait_send()


def per_device(n_row, n_col, tangent, block_row, block_col, tile_count, old_basis, old_id, residual):
    stored = tangent.shape[2]
    tile_rows = 2 * n_col
    tile_cols = 2 * n_row
    small = tile_cols <= 8
    vmem = pl.BlockSpec(memory_space=pltpu.VMEM)
    dma = pltpu.SemaphoreType.DMA
    c16, u16, coef = pl.pallas_call(
        functools.partial(kernel, n_row, n_col, tile_rows, tile_cols),
        out_shape=(
            jax.ShapeDtypeStruct((2 * OCT, WIDE), BF16),
            jax.ShapeDtypeStruct((2 * OCT, WIDE), BF16),
            jax.ShapeDtypeStruct((1, 128), F32),
        ),
        in_specs=[pl.BlockSpec(memory_space=pl.ANY), vmem, vmem, vmem, vmem,
                  pl.BlockSpec(memory_space=pltpu.SMEM), vmem],
        out_specs=(vmem, vmem, vmem),
        scratch_shapes=[
            pltpu.VMEM((stored, BLK * BLK), BF16),
            pltpu.VMEM((2 * OCT, WIDE), BF16),
            pltpu.VMEM((n_row, 2 * OCT, WIDE), BF16),
            pltpu.VMEM((tile_cols * 256, 256), BF16),
            pltpu.VMEM((4 * OCT * tile_rows, tile_cols * 256) if small else (16, 128), BF16),
            pltpu.VMEM((3, OCT * tile_rows, 128), F32),
            pltpu.VMEM((n_col, 3, 2 * OCT, 128), F32),
            pltpu.VMEM((n_row, 24, 128), F32),
            pltpu.VMEM((n_col, 24, 128), F32),
            dma, dma((n_row,)), dma((n_row,)), dma((n_col,)), dma((n_col,)),
            dma((n_row,)), dma((n_row,)), dma((n_col,)), dma((n_col,)),
        ],
        compiler_params=pltpu.CompilerParams(
            collective_id=0, has_side_effects=True, vmem_limit_bytes=40 * 1024 * 1024),
        name="refresh",
    )(tangent, block_row.reshape(1, stored), block_col.reshape(1, stored), tile_count.reshape(1, 1),
      old_basis, old_id, residual.reshape(1, 2 * BLK))
    return c16.reshape(2, BLK * K), u16.reshape(2, BLK * K), coef[0, :K]


def solution(mesh):
    return jax.shard_map(
        functools.partial(per_device, mesh.shape["row"], mesh.shape["col"]),
        mesh=mesh,
        in_specs=(
            P("row", "col", None, None),
            P("row", "col", None),
            P("row", "col", None),
            P("row", "col"),
            P(("row", "col"), None),
            P(("row", "col")),
            P(("row", "col")),
        ),
        out_specs=(P(("row", "col"), None), P(("row", "col"), None), P()),
        check_vma=False,
    )
```

time: 204 us -> 39 us (0.19)
  blocking collectives: 84.7 us -> 0 us
  waiting for transfers between devices: 71.4 us -> 0 us
  Pallas kernels: 0 us -> 33.3 us
  between operations: 15.5 us -> 1.32 us
  other arithmetic: 13.6 us -> 0 us
  local copies, waits for them, and re-layouts: 10.8 us -> 4.15 us
  starting transfers between devices: 4.58 us -> 0 us
  matrix products: 3.01 us -> 0 us
    psum x2 -> x0, blocking collectives: 79.5 us -> none  [the longest x1 39.9 us: per_device(): lax.psum(jnp.dot(ortho_t, residual, precision=highest), ('row', 'col'))]
    unnamed x2 -> x0, waiting for transfers between devices: 67.4 us -> none
    pallas_call x0 -> x1, Pallas kernels: none -> 33.3 us  [per_device(): pl.pallas_call(functools.partial(kernel, n_row, n_col, tile_rows, tile_co...]
    another operation x5 -> x0, other arithmetic: 9.38 us -> none  [the longest x3 5.05 us: per_device(): lower = jnp.linalg.cholesky(gram / jnp.float32(total_rows))]
    all_gather x1 -> x0, blocking collectives: 5.23 us -> none  [per_device(): col_basis = lax.all_gather(placed, 'row', axis=0, tiled=True)]
    ppermute x2 -> x0, starting transfers between devices: 4.54 us -> none  [passed_along(): lax.ppermute(array, axis, [(i, (i + by) % peers) for i in range(peers)])]
    ppermute x2 -> x0, waiting for transfers between devices: 4.01 us -> none  [passed_along(): lax.ppermute(array, axis, [(i, (i + by) % peers) for i in range(peers)])]
    dot_general x4 -> x0, matrix products: 2.47 us -> none  [the longest x1 1.88 us: add_group(): jnp.einsum('gij,gjk->gik', block_vals, picked, preferred_element_type=jnp...]
  transfers between devices with their start and end apart: 3 -> 0, of which waited for: 2 -> 0; matrix products, arithmetic and copies ran while one was open for 1% -> 0% of each run, Pallas kernels for 0% -> 0%
where the time goes in v1:
time: 39 us; the launch traced here: 38.7 us
  Pallas kernels  33.3 us (85%)
  local copies, waits for them, and re-layouts  4.15 us (11%)
  between operations  1.32 us (3%)
    pallas_call x1, Pallas kernels, per_device(): pl.pallas_call(functools.partial(kernel, n_row, n_col, tile_rows, tile_co...  33.3 us
    unnamed x12, local copies, waits for them, and re-layouts  2.42 us
    reshape x2, local copies, waits for them, and re-layouts, per_device(): return (c16.reshape(2, BLK * K), u16.reshape(2, BLK * K), coef[0, :K])  1.22 us

profile of v1, /device:TPU:0, one launch (start us, length us, event | category | flops | bytes accessed | tf_op | source)
XLA Modules:
  0.0 38.7 jit_solution(15622411766050777515)
XLA Ops:
  1.3 0.0 copy-start.5
  1.3 0.0 copy-start.2
  1.3 0.0 copy-start.3
  1.3 0.0 copy-start.4
  1.3 0.6 %copy-done.5 = f32[128]{0:T(128)S(1)} copy-done((f32[128]{0:T(128)S(1)}, f32[128]{0:T(128)}, u32[]{:S(2)}) %copy-start.5) | copy-done | bytes 536
  1.9 0.0 copy-done.2
  1.9 0.0 copy-done.3
  2.0 0.0 copy-done.4
  2.0 0.0 copy-start
  2.0 1.0 %copy-done = bf16[1,1,64,4096]{3,2,1,0:T(8,128)(2,1)S(1)} copy-done((bf16[1,1,64,4096]{3,2,1,0:T(8,128)(2,1)S(1)}, bf16[1,1,64,4096]{3,2,1,0:T(8,128)(2,1)}, u32[]{:S(2)}) %copy-start) | copy-done | bytes 524312
  3.0 0.0 copy-start.1
  3.0 0.7 %copy-done.1 = bf16[2,3072]{1,0:T(2,128)(2,1)S(1)} copy-done((bf16[2,3072]{1,0:T(2,128)(2,1)S(1)}, bf16[2,3072]{1,0:T(2,128)(2,1)}, u32[]{:S(2)}) %copy-start.1) | copy-done | bytes 12312
  3.7 33.3 %refresh.1 = (bf16[16,384]{1,0:T(8,128)(2,1)S(1)}, bf16[16,384]{1,0:T(8,128)(2,1)S(1)}, f32[1,128]{1,0:T(1,128)S(1)}) custom-call(bf16[1,1,64,4096]{3,2,1,0:T(8,128)(2,1)S(1)} %copy-done, s32[1,64]{1,0:T(1,128)S(1)} %bitcast.5, s32[1,64]{1,0:T(1,128)S(1)} %bitcast.6, s32[1,1]{1,0:T(1,128)S(6)} %copy.10.count_ref, bf16[2,3072]{1,0:T(2,128)(2,1)S(1)} %copy-done.1, ...), custom_call_target="tpu_custom_call" | custom-call | tf_op jit(solution)/shard_map/refresh/pallas_call | solution.py:273
  37.0 0.6 %reshape.24 = bf16[2,3072]{1,0:T(2,128)(2,1)} reshape(bf16[16,384]{1,0:T(8,128)(2,1)S(1)} %get-tuple-element.6) | data formatting | bytes 24576 | tf_op jit(solution)/shard_map/reshape | solution.py:301
  37.6 0.5 %slice_bitcast_fusion = f32[48]{0:T(128)} fusion(f32[1,128]{1,0:T(1,128)S(1)} %get-tuple-element.8), kind=kLoop, calls=%fused_computation | loop fusion | bytes 384 | tf_op jit(solution)/shard_map/squeeze | solution.py:301
  38.1 0.6 %reshape.25 = bf16[2,3072]{1,0:T(2,128)(2,1)} reshape(bf16[16,384]{1,0:T(8,128)(2,1)S(1)} %get-tuple-element.7) | data formatting | bytes 24576 | tf_op jit(solution)/shard_map/reshape | solution.py:301
Async XLA Ops:
  1.3 0.7 %copy-start.5 = (f32[128]{0:T(128)S(1)}, f32[128]{0:T(128)}, u32[]{:S(2)}) copy-start(f32[128]{0:T(128)} %param.13) | copy-start | bytes 1540
  1.3 0.7 %copy-start.2 = (s32[1,1,64]{2,1,0:T(1,128)S(1)}, s32[1,1,64]{2,1,0:T(1,128)}, u32[]{:S(2)}) copy-start(s32[1,1,64]{2,1,0:T(1,128)} %param.8) | copy-start | bytes 772
  1.3 0.7 %copy-start.3 = (s32[1,1,64]{2,1,0:T(1,128)S(1)}, s32[1,1,64]{2,1,0:T(1,128)}, u32[]{:S(2)}) copy-start(s32[1,1,64]{2,1,0:T(1,128)} %param.9) | copy-start | bytes 772
  1.3 0.7 %copy-start.4 = (s32[2]{0:T(128)S(1)}, s32[2]{0:T(128)}, u32[]{:S(2)}) copy-start(s32[2]{0:T(128)} %id_ref.1) | copy-start | bytes 28
  2.0 1.0 %copy-start = (bf16[1,1,64,4096]{3,2,1,0:T(8,128)(2,1)S(1)}, bf16[1,1,64,4096]{3,2,1,0:T(8,128)(2,1)}, u32[]{:S(2)}) copy-start(bf16[1,1,64,4096]{3,2,1,0:T(8,128)(2,1)} %tan_hbm.1) | copy-start | bytes 1572868
  3.0 0.7 %copy-start.1 = (bf16[2,3072]{1,0:T(2,128)(2,1)S(1)}, bf16[2,3072]{1,0:T(2,128)(2,1)}, u32[]{:S(2)}) copy-start(bf16[2,3072]{1,0:T(2,128)(2,1)} %basis_ref.1) | copy-start | bytes 36868

commit v2 on v1

--- a/solution.py
+++ b/solution.py
@@ -37,10 +37,10 @@
     return hi, mid, lo
 
 
-def kernel(n_row, n_col, tile_rows, tile_cols, tan_hbm, rows_ref, cols_ref, count_ref, basis_ref, id_ref, res_ref,
-           c_ref, u_ref, coef_ref,
-           tan, xs, xr, w, a, ps, pr, ga, gb,
-           tan_sem, bs_send, bs_recv, p_send, p_recv, ga_send, ga_recv, gb_send, gb_recv):
+def kernel(n_row, n_col, tile_rows, tile_cols, tan_hbm, rows_hbm, cols_hbm, count_hbm, basis_hbm, id_hbm,
+           res_hbm, product_ref, own_ref, gram_ref,
+           tan, rows_ref, cols_ref, count_ref, basis_ref, id_ref, res_ref, xs, xr, w, a, ps, pr, ga, gb,
+           load_sem, bs_send, bs_recv, p_send, p_recv, ga_send, ga_recv, gb_send, gb_recv):
     r = lax.axis_index("row")
     c = lax.axis_index("col")
     nxt = lax.rem(c + 1, n_col)
@@ -48,8 +48,11 @@
     small = tile_cols <= 8
     total = n_row * n_col * 2 * BLK
 
-    load = pltpu.make_async_copy(tan_hbm.at[0, 0], tan, tan_sem)
-    load.start()
+    loads = [pltpu.make_async_copy(src, dst, load_sem.at[n]) for n, (src, dst) in enumerate((
+        (basis_hbm, basis_ref), (id_hbm, id_ref), (tan_hbm.at[0, 0], tan), (rows_hbm, rows_ref),
+        (cols_hbm, cols_ref), (count_hbm, count_ref), (res_hbm, res_ref)))]
+    for load in loads:
+        load.start()
 
     barrier = pltpu.get_barrier_semaphore()
     greeted = 0
@@ -62,6 +65,8 @@
         pl.semaphore_signal(barrier, inc=1, device_id=(r, lax.rem(c + d, n_col)), device_id_type=MESH)
         greeted += 1
 
+    loads[0].wait()
+    loads[1].wait()
     flat = basis_ref[...].astype(F32)
     held = [jnp.concatenate([flat[s:s + 1, WIDE * g:WIDE * (g + 1)] for g in range(OCT)], axis=0) for s in range(2)]
     swapped = jnp.full((OCT, WIDE), id_ref[0] & 1, jnp.int32) == 1
@@ -79,20 +84,24 @@
         copy.start()
         basis_out.append(copy)
 
-    load.wait()
+    for load in loads[2:]:
+        load.wait()
     stored = tan.shape[0]
-    place = cols_ref[...] * tile_rows + rows_ref[...]
-    place = jnp.where(iota((1, stored), 1) < count_ref[...], place, -1)
-
-    def dense(first, many, g):
-        hot = (iota((many, stored), 0) + first == place).astype(F32).astype(BF16)
+    place = cols_ref[0] * tile_rows + rows_ref[0]
+    place = jnp.where(iota((1, stored), 1) < count_ref[0, 0], place, -1)
+
+    def live(first, many):
+        return (iota((many, stored), 0) + first == place).astype(F32).astype(BF16)
+
+    def dense(hot, g):
         d = jnp.dot(hot, tan[:, 512 * g:512 * (g + 1)], preferred_element_type=F32)
         hi = d.astype(BF16)
         return hi, (d - hi.astype(F32)).astype(BF16)
 
     if small:
+        hot = live(0, tile_cols * tile_rows)
         for g in range(OCT):
-            both = dense(0, tile_cols * tile_rows, g)
+            both = dense(hot, g)
             for part in range(2):
                 for h in range(2):
                     at = ((part * 2 + h) * OCT + g) * tile_rows
@@ -111,15 +120,11 @@
 
     own = iota((128, 128), 0)
     wanted = (own & 15) * 8 + lax.shift_right_logical(own, 4)
-    res_rows = jnp.where(iota((128, 128), 1) == wanted, jnp.broadcast_to(res_ref[...], (128, 128)), 0.0)
+    res_rows = jnp.where(iota((128, 128), 1) == wanted, jnp.broadcast_to(res_ref[...].reshape(1, 128), (128, 128)), 0.0)
     at_k = (iota((128, 128), 1) == K).astype(F32).astype(BF16)
     res_col = jnp.zeros((128, 128), F32)
     for piece in reversed(pieces(res_rows)):
         res_col += jnp.dot(piece, at_k, preferred_element_type=F32)
-    tile_row = iota((128, WIDE), 0)
-    tile_col = iota((128, WIDE), 1)
-    tile = (tile_row - SIDE == tile_col - K * over_k(tile_col, 8)).astype(F32).astype(BF16)
-
     for q in range(n_row):
         pltpu.make_async_remote_copy(
             src_ref=xs, dst_ref=xr.at[q], send_sem=bs_send.at[0], recv_sem=bs_recv.at[q],
@@ -152,7 +157,7 @@
     else:
         for g in range(OCT):
             def add(j, acc, g=g):
-                hi, lo = dense(j * tile_rows, tile_rows, g)
+                hi, lo = dense(live(j * tile_rows, tile_rows), g)
                 lhs = jnp.concatenate([hi[:, :256], hi[:, 256:], lo[:, :256], lo[:, 256:]], axis=0)
                 return acc + jnp.dot(lhs, w[pl.ds(pl.multiple_of(j * 256, 256), 256), :], preferred_element_type=F32)
             acc = lax.fori_loop(0, tile_cols, add, jnp.zeros((4 * tile_rows, 256), F32))
@@ -184,68 +189,103 @@
                            preferred_element_type=F32)
     packed = gram[:24] + pltpu.roll(gram[24:48], SIDE, 1)
 
-    ga[r] = packed
+    pair, side = c // 2, lax.rem(c, 2)
+    place_a = r * 2 + side
+    ga[place_a] = packed
     sent = []
-    for d in range(1, n_row):
-        to = lax.rem(r + d, n_row)
+    others = []
+    for d in range(2 * n_row):
+        if d:
+            row_to = lax.rem(r + d // 2, n_row)
+            side_to = lax.rem(side + d % 2, 2)
+            others.append((row_to * 2 + side_to, row_to, pair * 2 + side_to))
+    for d, (slot, row_to, col_to) in enumerate(others):
         copy = pltpu.make_async_remote_copy(
-            src_ref=ga.at[r], dst_ref=ga.at[r], send_sem=ga_send.at[d], recv_sem=ga_recv.at[r],
-            device_id=(to, c), device_id_type=MESH)
+            src_ref=ga.at[place_a], dst_ref=ga.at[place_a], send_sem=ga_send.at[d], recv_sem=ga_recv.at[place_a],
+            device_id=(row_to, col_to), device_id_type=MESH)
         copy.start()
         sent.append(copy)
-    for d in range(1, n_row):
-        source = lax.rem(r + d, n_row)
+    for d, (slot, row_to, col_to) in enumerate(others):
         pltpu.make_async_remote_copy(
-            src_ref=ga.at[r], dst_ref=ga.at[source], send_sem=ga_send.at[d], recv_sem=ga_recv.at[source],
-            device_id=(source, c), device_id_type=MESH).wait_recv()
+            src_ref=ga.at[place_a], dst_ref=ga.at[slot], send_sem=ga_send.at[d], recv_sem=ga_recv.at[slot],
+            device_id=(row_to, col_to), device_id_type=MESH).wait_recv()
     packed = ga[0]
-    for q in range(1, n_row):
+    for q in range(1, 2 * n_row):
         packed += ga[q]
-    gb[c] = packed
-    for d in range(1, n_col):
-        to = lax.rem(c + d, n_col)
+    gb[pair] = packed
+    pairs = n_col // 2
+    for d in range(1, pairs):
+        to = lax.rem(pair + d, pairs) * 2 + side
         copy = pltpu.make_async_remote_copy(
-            src_ref=gb.at[c], dst_ref=gb.at[c], send_sem=gb_send.at[d], recv_sem=gb_recv.at[c],
+            src_ref=gb.at[pair], dst_ref=gb.at[pair], send_sem=gb_send.at[d], recv_sem=gb_recv.at[pair],
             device_id=(r, to), device_id_type=MESH)
         copy.start()
         sent.append(copy)
-    for d in range(1, n_col):
-        source = lax.rem(c + d, n_col)
+    product_ref[...] = product
+    own_ref[...] = xr[r]
+    for d in range(1, pairs):
+        source = lax.rem(pair + d, pairs)
         pltpu.make_async_remote_copy(
-            src_ref=gb.at[c], dst_ref=gb.at[source], send_sem=gb_send.at[d], recv_sem=gb_recv.at[source],
-            device_id=(r, source), device_id_type=MESH).wait_recv()
+            src_ref=gb.at[pair], dst_ref=gb.at[source], send_sem=gb_send.at[d], recv_sem=gb_recv.at[source],
+            device_id=(r, source * 2 + side), device_id_type=MESH).wait_recv()
     packed = gb[0]
-    for q in range(1, n_col):
+    for q in range(1, pairs):
         packed += gb[q]
-
+    gram_ref[...] = packed
+
+    for copy in basis_out + prod_out + sent:
+        copy.wait_send()
+
+
+def eliminate(tiles):
+    sub = iota((8, 128), 0)
+    done = []
+    for t0 in range(K // 8):
+        j = 8 * t0
+        cols = [[jnp.broadcast_to(tiles[t][:, j + k:j + k + 1], (8, 128)) for t in range(t0, K // 8)] for k in range(8)]
+        rows = [jnp.broadcast_to(tiles[t0][i:i + 1, :], (8, 128)) for i in range(8)]
+        s = [[jnp.broadcast_to(cols[k][0][i:i + 1, :], (8, 128)) if i >= k else None for k in range(8)] for i in range(8)]
+        inv = []
+        scale = jnp.zeros((8, 128), F32)
+        for k in range(8):
+            inv.append(1.0 / s[k][k])
+            scale = jnp.where(sub == k, lax.rsqrt(s[k][k]), scale)
+            for i in range(k + 1, 8):
+                low = s[i][k] * inv[k]
+                rows[i] = rows[i] - low * rows[k]
+                for n in range(1, K // 8 - t0):
+                    cols[i][n] = cols[i][n] - cols[k][n] * low
+                for i2 in range(i, 8):
+                    s[i2][i] = s[i2][i] - s[i2][k] * low
+        for n in range(1, K // 8 - t0):
+            gone = cols[0][n] * (rows[0] * inv[0])
+            for k in range(1, 8):
+                gone = gone + cols[k][n] * (rows[k] * inv[k])
+            tiles[t0 + n] = tiles[t0 + n] - gone
+        mixed = rows[0]
+        for k in range(1, 8):
+            mixed = jnp.where(sub == k, rows[k], mixed)
+        done.append(mixed * scale)
+    return jnp.concatenate(done, axis=0)
+
+
+def finish(total, product_ref, own_ref, gram_ref, c_ref, u_ref, coef_ref):
     row_id = iota((K, 128), 0)
     lane_id = iota((K, 128), 1)
-    packed = packed * F32(1.0 / total)
+    packed = gram_ref[...] * F32(1.0 / total)
     m = jnp.concatenate([packed, pltpu.roll(packed, SIDE, 1)], axis=0)
     m = jnp.where(lane_id < SIDE, m, (lane_id - SIDE == row_id).astype(F32))
-    tiles = [m[8 * t:8 * (t + 1)] for t in range(K // 8)]
-    sub = iota((8, 128), 0)
-    for j in range(K):
-        t0, s0 = j // 8, j % 8
-        row = jnp.broadcast_to(tiles[t0][s0:s0 + 1, :], (8, 128))
-        inv = 1.0 / jnp.broadcast_to(tiles[t0][s0:s0 + 1, j:j + 1], (8, 128))
-        scaled = row * inv
-        for t in range(t0, K // 8):
-            if t == t0 and s0 == 7:
-                continue
-            col = jnp.broadcast_to(tiles[t][:, j:j + 1], (8, 128))
-            if t == t0:
-                col = jnp.where(sub > s0, col, 0.0)
-            tiles[t] = tiles[t] - col * scaled
-    m = jnp.concatenate(tiles, axis=0)
-    pivots = jnp.sum(jnp.where(lane_id == row_id, m, 0.0), axis=1, keepdims=True)
-    m = m * lax.rsqrt(jnp.broadcast_to(pivots, (K, 128)))
+    m = eliminate([m[8 * t:8 * (t + 1)] for t in range(K // 8)])
     coef = jnp.broadcast_to(m[:, K:K + 1], (K, 128)) * F32(math.sqrt(total))
-    coef_ref[...] = jnp.sum(jnp.where(lane_id == row_id, coef, 0.0), axis=0, keepdims=True)
-
+    coef_ref[...] = jnp.sum(jnp.where(lane_id == row_id, coef, 0.0), axis=0, keepdims=True)[:, :K]
+
+    tile_row = iota((128, WIDE), 0)
+    tile_col = iota((128, WIDE), 1)
+    tile = (tile_row - SIDE == tile_col - K * over_k(tile_col, 8)).astype(F32).astype(BF16)
+    mine = 2 * OCT
     inverse = jnp.where(lane_id >= SIDE, m, 0.0)
     diag_row = over_k(iota((K, WIDE), 1), 8)
-    left = jnp.concatenate(list(pieces(product)) + [xr[r]], axis=0)
+    left = jnp.concatenate(list(pieces(product_ref[...])) + [own_ref[...]], axis=0)
     acc = [None, None]
     for n, piece in enumerate(pieces(inverse)):
         wide = jnp.dot(piece, tile, preferred_element_type=F32)
@@ -256,11 +296,10 @@
             c_part = c_part + out[extra * mine:(extra + 1) * mine]
         u_part = out[3 * mine:4 * mine]
         acc = [c_part, u_part] if n == 0 else [acc[0] + c_part, acc[1] + u_part]
-    c_ref[...] = acc[0].astype(BF16)
-    u_ref[...] = acc[1].astype(BF16)
-
-    for copy in basis_out + prod_out + sent:
-        copy.wait_send()
+    for ref, whole in ((c_ref, acc[0]), (u_ref, acc[1])):
+        ref[...] = jnp.concatenate(
+            [jnp.concatenate([whole[g:g + 1], whole[OCT + g:OCT + g + 1]], axis=0) for g in range(OCT)], axis=1
+        ).astype(BF16)
 
 
 def per_device(n_row, n_col, tangent, block_row, block_col, tile_count, old_basis, old_id, residual):
@@ -270,35 +309,51 @@
     small = tile_cols <= 8
     vmem = pl.BlockSpec(memory_space=pltpu.VMEM)
     dma = pltpu.SemaphoreType.DMA
-    c16, u16, coef = pl.pallas_call(
+    product, own, gram = pl.pallas_call(
         functools.partial(kernel, n_row, n_col, tile_rows, tile_cols),
         out_shape=(
+            jax.ShapeDtypeStruct((2 * OCT, WIDE), F32),
             jax.ShapeDtypeStruct((2 * OCT, WIDE), BF16),
-            jax.ShapeDtypeStruct((2 * OCT, WIDE), BF16),
-            jax.ShapeDtypeStruct((1, 128), F32),
+            jax.ShapeDtypeStruct((24, 128), F32),
         ),
-        in_specs=[pl.BlockSpec(memory_space=pl.ANY), vmem, vmem, vmem, vmem,
-                  pl.BlockSpec(memory_space=pltpu.SMEM), vmem],
+        in_specs=[pl.BlockSpec(memory_space=pltpu.HBM)] * 7,
         out_specs=(vmem, vmem, vmem),
         scratch_shapes=[
             pltpu.VMEM((stored, BLK * BLK), BF16),
+            pltpu.VMEM((1, 1, stored), jnp.int32),
+            pltpu.VMEM((1, 1, stored), jnp.int32),
+            pltpu.SMEM((1, 1), jnp.int32),
+            pltpu.VMEM((2, BLK * K), BF16),
+            pltpu.SMEM((2,), jnp.int32),
+            pltpu.VMEM((2 * BLK,), F32),
             pltpu.VMEM((2 * OCT, WIDE), BF16),
             pltpu.VMEM((n_row, 2 * OCT, WIDE), BF16),
             pltpu.VMEM((tile_cols * 256, 256), BF16),
             pltpu.VMEM((4 * OCT * tile_rows, tile_cols * 256) if small else (16, 128), BF16),
             pltpu.VMEM((3, OCT * tile_rows, 128), F32),
             pltpu.VMEM((n_col, 3, 2 * OCT, 128), F32),
-            pltpu.VMEM((n_row, 24, 128), F32),
-            pltpu.VMEM((n_col, 24, 128), F32),
-            dma, dma((n_row,)), dma((n_row,)), dma((n_col,)), dma((n_col,)),
-            dma((n_row,)), dma((n_row,)), dma((n_col,)), dma((n_col,)),
+            pltpu.VMEM((2 * n_row, 24, 128), F32),
+            pltpu.VMEM((n_col // 2, 24, 128), F32),
+            dma((7,)), dma((n_row,)), dma((n_row,)), dma((n_col,)), dma((n_col,)),
+            dma((2 * n_row,)), dma((2 * n_row,)), dma((n_col // 2,)), dma((n_col // 2,)),
         ],
         compiler_params=pltpu.CompilerParams(
-            collective_id=0, has_side_effects=True, vmem_limit_bytes=40 * 1024 * 1024),
-        name="refresh",
-    )(tangent, block_row.reshape(1, stored), block_col.reshape(1, stored), tile_count.reshape(1, 1),
-      old_basis, old_id, residual.reshape(1, 2 * BLK))
-    return c16.reshape(2, BLK * K), u16.reshape(2, BLK * K), coef[0, :K]
+            collective_id=0, has_side_effects=True, vmem_limit_bytes=64 * 1024 * 1024),
+        name="reduce",
+    )(tangent, block_row, block_col, tile_count, old_basis, old_id, residual)
+    recycled_c, recycled_u, coefficients = pl.pallas_call(
+        functools.partial(finish, n_row * n_col * 2 * BLK),
+        out_shape=(
+            jax.ShapeDtypeStruct((2, BLK * K), BF16),
+            jax.ShapeDtypeStruct((2, BLK * K), BF16),
+            jax.ShapeDtypeStruct((1, K), F32),
+        ),
+        in_specs=[vmem] * 3,
+        out_specs=(vmem, vmem, vmem),
+        compiler_params=pltpu.CompilerParams(vmem_limit_bytes=16 * 1024 * 1024),
+        name="finish",
+    )(product, own, gram)
+    return recycled_c, recycled_u, coefficients[0]
 
 
 def solution(mesh):

time: 39 us -> 32.8 us (0.84)
  Pallas kernels: 33.3 us -> 29 us
  local copies, waits for them, and re-layouts: 4.15 us -> 2.14 us
    pallas_call x1, Pallas kernels: 33.3 us -> 26.3 us  [per_device(): pl.pallas_call(functools.partial(kernel, n_row, n_col, tile_rows, tile_co...]
    pallas_call x0 -> x1, Pallas kernels: none -> 2.7 us  [per_device(): pl.pallas_call(functools.partial(finish, n_row * n_col * 2 * BLK), out_sh...]
    reshape x2 -> x0, local copies, waits for them, and re-layouts: 1.22 us -> none  [per_device(): return (c16.reshape(2, BLK * K), u16.reshape(2, BLK * K), coef[0, :K])]
    squeeze x1 -> x0, local copies, waits for them, and re-layouts: 0.51 us -> none  [per_device(): return (c16.reshape(2, BLK * K), u16.reshape(2, BLK * K), coef[0, :K])]
    unnamed x12 -> x6, local copies, waits for them, and re-layouts: 2.42 us -> 2.14 us
where the time goes in v2:
time: 32.8 us; the launch traced here: 32.4 us
  Pallas kernels  29 us (88%)
  local copies, waits for them, and re-layouts  2.14 us (7%)
  between operations  1.3 us (4%)
    pallas_call x1, Pallas kernels, per_device(): pl.pallas_call(functools.partial(kernel, n_row, n_col, tile_rows, tile_co...  26.3 us
    pallas_call x1, Pallas kernels, per_device(): pl.pallas_call(functools.partial(finish, n_row * n_col * 2 * BLK), out_sh...  2.7 us
    unnamed x6, local copies, waits for them, and re-layouts  2.14 us

profile of v2, /device:TPU:0, one launch (start us, length us, event | category | flops | bytes accessed | tf_op | source)
XLA Modules:
  0.0 32.4 jit_solution(10818143853998843475)
XLA Ops:
  1.3 26.3 %reduce.1 = (f32[16,384]{1,0:T(8,128)}, bf16[16,384]{1,0:T(8,128)(2,1)}, f32[24,128]{1,0:T(8,128)}) custom-call(bf16[1,1,64,4096]{3,2,1,0:T(8,128)(2,1)} %tan_hbm.1, s32[1,1,64]{2,1,0:T(1,128)} %rows_hbm.1, s32[1,1,64]{2,1,0:T(1,128)} %cols_hbm.1, s32[1,1]{1,0:T(1,128)S(6)} %copy.10.count_hbm, bf16[2,3072]{1,0:T(2,128)(2,1)} %basis_hbm.1, s32[2]{0:T(128)} %id_hbm.1, ...), custom_call_target="tpu_custom_call" | custom-call | tf_op jit(solution)/shard_map/reduce/pallas_call | solution.py:312
  27.5 0.0 copy-start
  27.5 0.7 %copy-done = f32[16,384]{1,0:T(8,128)S(1)} copy-done((f32[16,384]{1,0:T(8,128)S(1)}, f32[16,384]{1,0:T(8,128)}, u32[]{:S(2)}) %copy-start) | copy-done | bytes 24600
  28.3 0.0 copy-start.1
  28.3 0.7 %copy-done.1 = bf16[16,384]{1,0:T(8,128)(2,1)S(1)} copy-done((bf16[16,384]{1,0:T(8,128)(2,1)S(1)}, bf16[16,384]{1,0:T(8,128)(2,1)}, u32[]{:S(2)}) %copy-start.1) | copy-done | bytes 12312
  29.0 0.0 copy-start.2
  29.0 0.7 %copy-done.2 = f32[24,128]{1,0:T(8,128)S(1)} copy-done((f32[24,128]{1,0:T(8,128)S(1)}, f32[24,128]{1,0:T(8,128)}, u32[]{:S(2)}) %copy-start.2) | copy-done | bytes 12312
  29.7 2.7 %finish.1 = (bf16[2,3072]{1,0:T(2,128)(2,1)}, bf16[2,3072]{1,0:T(2,128)(2,1)}, f32[1,48]{1,0:T(1,128)}) custom-call(f32[16,384]{1,0:T(8,128)S(1)} %copy-done, bf16[16,384]{1,0:T(8,128)(2,1)S(1)} %copy-done.1, f32[24,128]{1,0:T(8,128)S(1)} %copy-done.2), custom_call_target="tpu_custom_call" | custom-call | tf_op jit(solution)/shard_map/finish/pallas_call | solution.py:344
Async XLA Ops:
  27.5 0.7 %copy-start = (f32[16,384]{1,0:T(8,128)S(1)}, f32[16,384]{1,0:T(8,128)}, u32[]{:S(2)}) copy-start(f32[16,384]{1,0:T(8,128)} %get-tuple-element.9.product_ref) | copy-start | bytes 73732
  28.3 0.7 %copy-start.1 = (bf16[16,384]{1,0:T(8,128)(2,1)S(1)}, bf16[16,384]{1,0:T(8,128)(2,1)}, u32[]{:S(2)}) copy-start(bf16[16,384]{1,0:T(8,128)(2,1)} %get-tuple-element.10.own_ref) | copy-start | bytes 36868
  29.0 0.7 %copy-start.2 = (f32[24,128]{1,0:T(8,128)S(1)}, f32[24,128]{1,0:T(8,128)}, u32[]{:S(2)}) copy-start(f32[24,128]{1,0:T(8,128)} %get-tuple-element.11.gram_ref) | copy-start | bytes 36868

commit v3 on v2

--- a/solution.py
+++ b/solution.py
@@ -38,15 +38,15 @@
 
 
 def kernel(n_row, n_col, tile_rows, tile_cols, tan_hbm, rows_hbm, cols_hbm, count_hbm, basis_hbm, id_hbm,
-           res_hbm, product_ref, own_ref, gram_ref,
+           res_hbm, out_ref,
            tan, rows_ref, cols_ref, count_ref, basis_ref, id_ref, res_ref, xs, xr, w, a, ps, pr, ga, gb,
            load_sem, bs_send, bs_recv, p_send, p_recv, ga_send, ga_recv, gb_send, gb_recv):
     r = lax.axis_index("row")
     c = lax.axis_index("col")
     nxt = lax.rem(c + 1, n_col)
     prv = lax.rem(c + n_col - 1, n_col)
-    small = tile_cols <= 8
-    total = n_row * n_col * 2 * BLK
+    small = tile_cols <= 8 and tile_rows == 16
+    lead = n_col // 4
 
     loads = [pltpu.make_async_copy(src, dst, load_sem.at[n]) for n, (src, dst) in enumerate((
         (basis_hbm, basis_ref), (id_hbm, id_ref), (tan_hbm.at[0, 0], tan), (rows_hbm, rows_ref),
@@ -87,7 +87,8 @@
     for load in loads[2:]:
         load.wait()
     stored = tan.shape[0]
-    place = cols_ref[0] * tile_rows + rows_ref[0]
+    turned_row = rows_ref[0] - 2 * lax.rem(c + lead, n_col)
+    place = cols_ref[0] * tile_rows + jnp.where(turned_row < 0, turned_row + tile_rows, turned_row)
     place = jnp.where(iota((1, stored), 1) < count_ref[0, 0], place, -1)
 
     def live(first, many):
@@ -95,19 +96,19 @@
 
     def dense(hot, g):
         d = jnp.dot(hot, tan[:, 512 * g:512 * (g + 1)], preferred_element_type=F32)
-        hi = d.astype(BF16)
-        return hi, (d - hi.astype(F32)).astype(BF16)
+        hi = d.astype(BF16).astype(F32)
+        return hi, d - hi
 
     if small:
         hot = live(0, tile_cols * tile_rows)
         for g in range(OCT):
-            both = dense(hot, g)
-            for part in range(2):
+            hi, lo = dense(hot, g)
+            for half in range(2):
                 for h in range(2):
-                    at = ((part * 2 + h) * OCT + g) * tile_rows
+                    at = ((half * 2 + h) * OCT + g) * 16
                     for j in range(tile_cols):
-                        a[at:at + tile_rows, 256 * j:256 * (j + 1)] = (
-                            both[part][tile_rows * j:tile_rows * (j + 1), 256 * h:256 * (h + 1)])
+                        take = (slice(16 * j + 8 * half, 16 * j + 8 * half + 8), slice(256 * h, 256 * (h + 1)))
+                        a[at:at + 16, 256 * j:256 * (j + 1)] = jnp.concatenate([hi[take], lo[take]], axis=0).astype(BF16)
 
     lane_k = over_k(iota((8, WIDE), 1), 8)
     own_lane = lane_k == iota((8, WIDE), 0)
@@ -118,13 +119,6 @@
         spread_col < 4 * K).astype(F32).astype(BF16)
     quarter = over_k(iota((BLK, 256), 1), 5)
 
-    own = iota((128, 128), 0)
-    wanted = (own & 15) * 8 + lax.shift_right_logical(own, 4)
-    res_rows = jnp.where(iota((128, 128), 1) == wanted, jnp.broadcast_to(res_ref[...].reshape(1, 128), (128, 128)), 0.0)
-    at_k = (iota((128, 128), 1) == K).astype(F32).astype(BF16)
-    res_col = jnp.zeros((128, 128), F32)
-    for piece in reversed(pieces(res_rows)):
-        res_col += jnp.dot(piece, at_k, preferred_element_type=F32)
     for q in range(n_row):
         pltpu.make_async_remote_copy(
             src_ref=xs, dst_ref=xr.at[q], send_sem=bs_send.at[0], recv_sem=bs_recv.at[q],
@@ -141,39 +135,53 @@
                 at = (2 * q + m) * 256 + e * BLK
                 w[at:at + BLK, :] = jnp.where(quarter == e, wide[BLK * m:BLK * (m + 1)], 0.0).astype(BF16)
 
-    def put(g, left, right):
+    def put(first, g, left, right):
         turned = pltpu.roll(right, 64, 1)
-        row = pl.ds(g, tile_rows, stride=OCT)
+        row = pl.ds(first * OCT + g, left.shape[0], stride=OCT)
         ps[0, row, :] = left[:, 0:128]
         ps[1, row, :] = left[:, 128:256] + turned[:, 0:128]
         ps[2, row, :] = turned[:, 128:256]
 
-    half = OCT * tile_rows
+    mine = 2 * OCT
+    prod_out = []
+
+    def send(places):
+        for p in sorted(places, key=lambda p: abs((p + lead) % n_col * 2 - n_col)):
+            d = (p + lead) % n_col
+            if d:
+                copy = pltpu.make_async_remote_copy(
+                    src_ref=ps.at[:, pl.ds(p * mine, mine)], dst_ref=pr.at[c],
+                    send_sem=p_send.at[d], recv_sem=p_recv.at[c], device_id=(r, lax.rem(c + d, n_col)),
+                    device_id_type=MESH)
+                copy.start()
+                prod_out.append(copy)
+
     if small:
-        prod = jnp.dot(a[...], w[...], preferred_element_type=F32)
-        prod = prod[:2 * half] + prod[2 * half:]
-        for g in range(OCT):
-            put(g, prod[tile_rows * g:tile_rows * (g + 1)], prod[half + tile_rows * g:half + tile_rows * (g + 1)])
+        for half in range(2):
+            prod = jnp.dot(a[256 * half:256 * (half + 1), :], w[...], preferred_element_type=F32)
+            slabs = [prod[16 * n:16 * n + 8] + prod[16 * n + 8:16 * n + 16] for n in range(2 * OCT)]
+            for g in range(OCT):
+                put(8 * half, g, slabs[g], slabs[OCT + g])
+            send(range(4 * half, 4 * half + 4))
     else:
         for g in range(OCT):
             def add(j, acc, g=g):
                 hi, lo = dense(live(j * tile_rows, tile_rows), g)
-                lhs = jnp.concatenate([hi[:, :256], hi[:, 256:], lo[:, :256], lo[:, 256:]], axis=0)
+                lhs = jnp.concatenate([hi[:, :256], hi[:, 256:], lo[:, :256], lo[:, 256:]], axis=0).astype(BF16)
                 return acc + jnp.dot(lhs, w[pl.ds(pl.multiple_of(j * 256, 256), 256), :], preferred_element_type=F32)
             acc = lax.fori_loop(0, tile_cols, add, jnp.zeros((4 * tile_rows, 256), F32))
             acc = acc[:2 * tile_rows] + acc[2 * tile_rows:]
-            put(g, acc[:tile_rows], acc[tile_rows:])
-
-    mine = 2 * OCT
-    prod_out = []
-    for d in range(1, n_col):
-        to = lax.rem(c + d, n_col)
-        copy = pltpu.make_async_remote_copy(
-            src_ref=ps.at[:, pl.ds(pl.multiple_of(to * mine, mine), mine)], dst_ref=pr.at[c],
-            send_sem=p_send.at[d], recv_sem=p_recv.at[c], device_id=(r, to), device_id_type=MESH)
-        copy.start()
-        prod_out.append(copy)
-    product = ps[:, pl.ds(pl.multiple_of(c * mine, mine), mine), :]
+            put(0, g, acc[:tile_rows], acc[tile_rows:])
+        send(range(n_col))
+
+    own = iota((128, 128), 0)
+    wanted = (own & 15) * 8 + lax.shift_right_logical(own, 4)
+    res_rows = jnp.where(iota((128, 128), 1) == wanted, jnp.broadcast_to(res_ref[...].reshape(1, 128), (128, 128)), 0.0)
+    at_k = (iota((128, 128), 1) == K).astype(F32).astype(BF16)
+    res_col = jnp.zeros((128, 128), F32)
+    for piece in reversed(pieces(res_rows)):
+        res_col += jnp.dot(piece, at_k, preferred_element_type=F32)
+    product = ps[:, (n_col - lead) * mine:(n_col - lead + 1) * mine, :]
     for d in range(1, n_col):
         source = lax.rem(c + d, n_col)
         pltpu.make_async_remote_copy(
@@ -187,7 +195,10 @@
     stacked = jnp.concatenate([jnp.where(lane < K, t[:, :128], 0.0) for t in turned], axis=0) + res_col
     gram = lax.dot_general(stacked, stacked, (((0,), (0,)), ((), ())), precision=lax.Precision.HIGHEST,
                            preferred_element_type=F32)
-    packed = gram[:24] + pltpu.roll(gram[24:48], SIDE, 1)
+    parts = [gram[16 * n:16 * (n + 1)] for n in range(3)]
+    packed = parts[0]
+    for first, n, by in ((16, 1, 16), (48, 2, 48), (96, 0, 48), (97, 1, 49), (98, 2, 50)):
+        packed = jnp.where(lane >= first, pltpu.roll(parts[n], by, 1), packed)
 
     pair, side = c // 2, lax.rem(c, 2)
     place_a = r * 2 + side
@@ -221,8 +232,10 @@
             device_id=(r, to), device_id_type=MESH)
         copy.start()
         sent.append(copy)
-    product_ref[...] = product
-    own_ref[...] = xr[r]
+    own = xr[r].astype(F32)
+    for t in range(3):
+        out_ref[16 * t:16 * (t + 1), :] = product[:, 128 * t:128 * (t + 1)]
+        out_ref[48 + 16 * t:64 + 16 * t, :] = own[:, 128 * t:128 * (t + 1)]
     for d in range(1, pairs):
         source = lax.rem(pair + d, pairs)
         pltpu.make_async_remote_copy(
@@ -231,7 +244,7 @@
     packed = gb[0]
     for q in range(1, pairs):
         packed += gb[q]
-    gram_ref[...] = packed
+    out_ref[96:112, :] = packed
 
     for copy in basis_out + prod_out + sent:
         copy.wait_send()
@@ -269,11 +282,15 @@
     return jnp.concatenate(done, axis=0)
 
 
-def finish(total, product_ref, own_ref, gram_ref, c_ref, u_ref, coef_ref):
+def finish(total, in_ref, c_ref, u_ref, coef_ref):
     row_id = iota((K, 128), 0)
     lane_id = iota((K, 128), 1)
-    packed = gram_ref[...] * F32(1.0 / total)
-    m = jnp.concatenate([packed, pltpu.roll(packed, SIDE, 1)], axis=0)
+    packed = in_ref[96:112, :] * F32(1.0 / total)
+    low = jnp.concatenate([packed if by == 0 else pltpu.roll(packed, 128 - by, 1) for by in (0, 16, 48)], axis=0)
+    beside = jnp.concatenate([pltpu.roll(packed, 128 - by, 1) for by in (48, 49, 50)], axis=0)
+    high = jnp.concatenate([low, jnp.zeros((128 - K, 128), F32)], axis=0).T[:K]
+    m = jnp.where(lane_id <= (row_id | 15), low, high)
+    m = jnp.where(lane_id == K, beside, m)
     m = jnp.where(lane_id < SIDE, m, (lane_id - SIDE == row_id).astype(F32))
     m = eliminate([m[8 * t:8 * (t + 1)] for t in range(K // 8)])
     coef = jnp.broadcast_to(m[:, K:K + 1], (K, 128)) * F32(math.sqrt(total))
@@ -285,7 +302,9 @@
     mine = 2 * OCT
     inverse = jnp.where(lane_id >= SIDE, m, 0.0)
     diag_row = over_k(iota((K, WIDE), 1), 8)
-    left = jnp.concatenate(list(pieces(product_ref[...])) + [own_ref[...]], axis=0)
+    product, own = (
+        jnp.concatenate([in_ref[first + 16 * t:first + 16 * (t + 1), :] for t in range(3)], axis=1) for first in (0, 48))
+    left = jnp.concatenate(list(pieces(product)) + [own.astype(BF16)], axis=0)
     acc = [None, None]
     for n, piece in enumerate(pieces(inverse)):
         wide = jnp.dot(piece, tile, preferred_element_type=F32)
@@ -306,18 +325,14 @@
     stored = tangent.shape[2]
     tile_rows = 2 * n_col
     tile_cols = 2 * n_row
-    small = tile_cols <= 8
+    small = tile_cols <= 8 and tile_rows == 16
     vmem = pl.BlockSpec(memory_space=pltpu.VMEM)
     dma = pltpu.SemaphoreType.DMA
-    product, own, gram = pl.pallas_call(
+    shares = pl.pallas_call(
         functools.partial(kernel, n_row, n_col, tile_rows, tile_cols),
-        out_shape=(
-            jax.ShapeDtypeStruct((2 * OCT, WIDE), F32),
-            jax.ShapeDtypeStruct((2 * OCT, WIDE), BF16),
-            jax.ShapeDtypeStruct((24, 128), F32),
-        ),
+        out_shape=jax.ShapeDtypeStruct((112, 128), F32),
         in_specs=[pl.BlockSpec(memory_space=pltpu.HBM)] * 7,
-        out_specs=(vmem, vmem, vmem),
+        out_specs=vmem,
         scratch_shapes=[
             pltpu.VMEM((stored, BLK * BLK), BF16),
             pltpu.VMEM((1, 1, stored), jnp.int32),
@@ -332,8 +347,8 @@
             pltpu.VMEM((4 * OCT * tile_rows, tile_cols * 256) if small else (16, 128), BF16),
             pltpu.VMEM((3, OCT * tile_rows, 128), F32),
             pltpu.VMEM((n_col, 3, 2 * OCT, 128), F32),
-            pltpu.VMEM((2 * n_row, 24, 128), F32),
-            pltpu.VMEM((n_col // 2, 24, 128), F32),
+            pltpu.VMEM((2 * n_row, 16, 128), F32),
+            pltpu.VMEM((n_col // 2, 16, 128), F32),
             dma((7,)), dma((n_row,)), dma((n_row,)), dma((n_col,)), dma((n_col,)),
             dma((2 * n_row,)), dma((2 * n_row,)), dma((n_col // 2,)), dma((n_col // 2,)),
         ],
@@ -348,11 +363,11 @@
             jax.ShapeDtypeStruct((2, BLK * K), BF16),
             jax.ShapeDtypeStruct((1, K), F32),
         ),
-        in_specs=[vmem] * 3,
+        in_specs=[vmem],
         out_specs=(vmem, vmem, vmem),
         compiler_params=pltpu.CompilerParams(vmem_limit_bytes=16 * 1024 * 1024),
         name="finish",
-    )(product, own, gram)
+    )(shares)
     return recycled_c, recycled_u, coefficients[0]
 
 

time: 32.8 us -> 31.1 us (0.948)
  local copies, waits for them, and re-layouts: 2.14 us -> 0.81 us
    unnamed x6 -> x2, local copies, waits for them, and re-layouts: 2.14 us -> 0.81 us
    pallas_call x1, Pallas kernels: 26.3 us -> 25.9 us  [per_device(): pl.pallas_call(functools.partial(kernel, n_row, n_col, tile_rows, tile_co...]
where the time goes in v3:
time: 31.1 us; the launch traced here: 30.9 us
  Pallas kernels  28.7 us (92%)
  between operations  1.29 us (4%)
  local copies, waits for them, and re-layouts  0.81 us (3%)
    pallas_call x1, Pallas kernels, per_device(): pl.pallas_call(functools.partial(kernel, n_row, n_col, tile_rows, tile_co...  25.9 us
    pallas_call x1, Pallas kernels, per_device(): pl.pallas_call(functools.partial(finish, n_row * n_col * 2 * BLK), out_sh...  2.85 us
    unnamed x2, local copies, waits for them, and re-layouts  0.81 us

profile of v3, /device:TPU:0, one launch (start us, length us, event | category | flops | bytes accessed | tf_op | source)
XLA Modules:
  0.0 30.9 jit_solution(3968485682472419059)
XLA Ops:
  1.3 25.9 %reduce.1.in_ref = f32[112,128]{1,0:T(8,128)} custom-call(bf16[1,1,64,4096]{3,2,1,0:T(8,128)(2,1)} %tan_hbm.1, s32[1,1,64]{2,1,0:T(1,128)} %rows_hbm.1, s32[1,1,64]{2,1,0:T(1,128)} %cols_hbm.1, s32[1,1]{1,0:T(1,128)S(6)} %copy.10.count_hbm, bf16[2,3072]{1,0:T(2,128)(2,1)} %basis_hbm.1, s32[2]{0:T(128)} %id_hbm.1, f32[128]{0:T(128)} %res_hbm.1), custom_call_target="tpu_custom_call" | custom-call | tf_op jit(solution)/shard_map/reduce/pallas_call | solution.py:331
  27.2 0.0 copy-start
  27.2 0.8 %copy-done = f32[112,128]{1,0:T(8,128)S(1)} copy-done((f32[112,128]{1,0:T(8,128)S(1)}, f32[112,128]{1,0:T(8,128)}, u32[]{:S(2)}) %copy-start) | copy-done | bytes 57368
  28.0 2.8 %finish.1 = (bf16[2,3072]{1,0:T(2,128)(2,1)}, bf16[2,3072]{1,0:T(2,128)(2,1)}, f32[1,48]{1,0:T(1,128)}) custom-call(f32[112,128]{1,0:T(8,128)S(1)} %copy-done), custom_call_target="tpu_custom_call" | custom-call | tf_op jit(solution)/shard_map/finish/pallas_call | solution.py:359
Async XLA Ops:
  27.2 0.8 %copy-start = (f32[112,128]{1,0:T(8,128)S(1)}, f32[112,128]{1,0:T(8,128)}, u32[]{:S(2)}) copy-start(f32[112,128]{1,0:T(8,128)} %reduce.1.in_ref) | copy-start | bytes 172036

commit v4 on v3

--- a/solution.py
+++ b/solution.py
@@ -65,6 +65,15 @@
         pl.semaphore_signal(barrier, inc=1, device_id=(r, lax.rem(c + d, n_col)), device_id_type=MESH)
         greeted += 1
 
+    lane_k = over_k(iota((8, WIDE), 1), 8)
+    own_lane = lane_k == iota((8, WIDE), 0)
+    spread_row = iota((WIDE, 256), 0)
+    spread_col = iota((WIDE, 256), 1)
+    spread = jnp.logical_and(
+        spread_row - K * over_k(spread_row, 8) == spread_col - K * over_k(spread_col, 4),
+        spread_col < 4 * K).astype(F32).astype(BF16)
+    quarter = over_k(iota((BLK, 256), 1), 5)
+
     loads[0].wait()
     loads[1].wait()
     flat = basis_ref[...].astype(F32)
@@ -109,15 +118,6 @@
                     for j in range(tile_cols):
                         take = (slice(16 * j + 8 * half, 16 * j + 8 * half + 8), slice(256 * h, 256 * (h + 1)))
                         a[at:at + 16, 256 * j:256 * (j + 1)] = jnp.concatenate([hi[take], lo[take]], axis=0).astype(BF16)
-
-    lane_k = over_k(iota((8, WIDE), 1), 8)
-    own_lane = lane_k == iota((8, WIDE), 0)
-    spread_row = iota((WIDE, 256), 0)
-    spread_col = iota((WIDE, 256), 1)
-    spread = jnp.logical_and(
-        spread_row - K * over_k(spread_row, 8) == spread_col - K * over_k(spread_col, 4),
-        spread_col < 4 * K).astype(F32).astype(BF16)
-    quarter = over_k(iota((BLK, 256), 1), 5)
 
     for q in range(n_row):
         pltpu.make_async_remote_copy(
@@ -193,8 +193,10 @@
     lane = iota((2 * OCT, 128), 1)
     turned = [product if b == 0 else pltpu.roll(product, WIDE - K * b, 1) for b in range(8)]
     stacked = jnp.concatenate([jnp.where(lane < K, t[:, :128], 0.0) for t in turned], axis=0) + res_col
-    gram = lax.dot_general(stacked, stacked, (((0,), (0,)), ((), ())), precision=lax.Precision.HIGHEST,
-                           preferred_element_type=F32)
+    hi, mid, lo = pieces(stacked)
+    gram = lax.dot_general(
+        jnp.concatenate([lo, hi, mid, mid, hi, hi], axis=0)[:, :SIDE],
+        jnp.concatenate([hi, lo, mid, hi, mid, hi], axis=0), (((0,), (0,)), ((), ())), preferred_element_type=F32)
     parts = [gram[16 * n:16 * (n + 1)] for n in range(3)]
     packed = parts[0]
     for first, n, by in ((16, 1, 16), (48, 2, 48), (96, 0, 48), (97, 1, 49), (98, 2, 50)):
@@ -282,9 +284,16 @@
     return jnp.concatenate(done, axis=0)
 
 
-def finish(total, in_ref, c_ref, u_ref, coef_ref):
+def finish(total, in_hbm, c_ref, u_ref, coef_ref, in_ref, sem):
+    load = pltpu.make_async_copy(in_hbm, in_ref, sem)
+    load.start()
     row_id = iota((K, 128), 0)
     lane_id = iota((K, 128), 1)
+    tile_row = iota((128, WIDE), 0)
+    tile_col = iota((128, WIDE), 1)
+    tile = (tile_row - SIDE == tile_col - K * over_k(tile_col, 8)).astype(F32).astype(BF16)
+    diag_row = over_k(iota((K, WIDE), 1), 8)
+    load.wait()
     packed = in_ref[96:112, :] * F32(1.0 / total)
     low = jnp.concatenate([packed if by == 0 else pltpu.roll(packed, 128 - by, 1) for by in (0, 16, 48)], axis=0)
     beside = jnp.concatenate([pltpu.roll(packed, 128 - by, 1) for by in (48, 49, 50)], axis=0)
@@ -296,12 +305,8 @@
     coef = jnp.broadcast_to(m[:, K:K + 1], (K, 128)) * F32(math.sqrt(total))
     coef_ref[...] = jnp.sum(jnp.where(lane_id == row_id, coef, 0.0), axis=0, keepdims=True)[:, :K]
 
-    tile_row = iota((128, WIDE), 0)
-    tile_col = iota((128, WIDE), 1)
-    tile = (tile_row - SIDE == tile_col - K * over_k(tile_col, 8)).astype(F32).astype(BF16)
     mine = 2 * OCT
     inverse = jnp.where(lane_id >= SIDE, m, 0.0)
-    diag_row = over_k(iota((K, WIDE), 1), 8)
     product, own = (
         jnp.concatenate([in_ref[first + 16 * t:first + 16 * (t + 1), :] for t in range(3)], axis=1) for first in (0, 48))
     left = jnp.concatenate(list(pieces(product)) + [own.astype(BF16)], axis=0)
@@ -363,9 +368,10 @@
             jax.ShapeDtypeStruct((2, BLK * K), BF16),
             jax.ShapeDtypeStruct((1, K), F32),
         ),
-        in_specs=[vmem],
+        in_specs=[pl.BlockSpec(memory_space=pltpu.HBM)],
         out_specs=(vmem, vmem, vmem),
-        compiler_params=pltpu.CompilerParams(vmem_limit_bytes=16 * 1024 * 1024),
+        scratch_shapes=[pltpu.VMEM((112, 128), F32), dma],
+        compiler_params=pltpu.CompilerParams(vmem_limit_bytes=64 * 1024 * 1024),
         name="finish",
     )(shares)
     return recycled_c, recycled_u, coefficients[0]

time: 31.1 us -> 31 us (level)
  local copies, waits for them, and re-layouts: 0.81 us -> 0 us
  Pallas kernels: 28.7 us -> 29.5 us
    pallas_call x1, Pallas kernels: 2.85 us -> 3.67 us  [per_device(): pl.pallas_call(functools.partial(finish, n_row * n_col * 2 * BLK), out_sh...]
    unnamed x2 -> x0, local copies, waits for them, and re-layouts: 0.81 us -> none
where the time goes in v4:
time: 31 us; the launch traced here: 30.8 us
  Pallas kernels  29.5 us (95%)
  between operations  1.29 us (4%)
    pallas_call x1, Pallas kernels, per_device(): pl.pallas_call(functools.partial(kernel, n_row, n_col, tile_rows, tile_co...  25.8 us
    pallas_call x1, Pallas kernels, per_device(): pl.pallas_call(functools.partial(finish, n_row * n_col * 2 * BLK), out_sh...  3.67 us

profile of v4, /device:TPU:0, one launch (start us, length us, event | category | flops | bytes accessed | tf_op | source)
XLA Modules:
  0.0 30.8 jit_solution(4460545378255555867)
XLA Ops:
  1.3 25.8 %reduce.1.in_hbm = f32[112,128]{1,0:T(8,128)} custom-call(bf16[1,1,64,4096]{3,2,1,0:T(8,128)(2,1)} %tan_hbm.1, s32[1,1,64]{2,1,0:T(1,128)} %rows_hbm.1, s32[1,1,64]{2,1,0:T(1,128)} %cols_hbm.1, s32[1,1]{1,0:T(1,128)S(6)} %copy.10.count_hbm, bf16[2,3072]{1,0:T(2,128)(2,1)} %basis_hbm.1, s32[2]{0:T(128)} %id_hbm.1, f32[128]{0:T(128)} %res_hbm.1), custom_call_target="tpu_custom_call" | custom-call | tf_op jit(solution)/shard_map/reduce/pallas_call | solution.py:336
  27.1 3.7 %finish.1 = (bf16[2,3072]{1,0:T(2,128)(2,1)}, bf16[2,3072]{1,0:T(2,128)(2,1)}, f32[1,48]{1,0:T(1,128)}) custom-call(f32[112,128]{1,0:T(8,128)} %reduce.1.in_hbm), custom_call_target="tpu_custom_call" | custom-call | tf_op jit(solution)/shard_map/finish/pallas_call | solution.py:364

commit v5 on v4

--- a/solution.py
+++ b/solution.py
@@ -358,7 +358,7 @@
             dma((2 * n_row,)), dma((2 * n_row,)), dma((n_col // 2,)), dma((n_col // 2,)),
         ],
         compiler_params=pltpu.CompilerParams(
-            collective_id=0, has_side_effects=True, vmem_limit_bytes=64 * 1024 * 1024),
+            collective_id=0, has_side_effects=True, vmem_limit_bytes=54900 * 1024),
         name="reduce",
     )(tangent, block_row, block_col, tile_count, old_basis, old_id, residual)
     recycled_c, recycled_u, coefficients = pl.pallas_call(
@@ -371,7 +371,7 @@
         in_specs=[pl.BlockSpec(memory_space=pltpu.HBM)],
         out_specs=(vmem, vmem, vmem),
         scratch_shapes=[pltpu.VMEM((112, 128), F32), dma],
-        compiler_params=pltpu.CompilerParams(vmem_limit_bytes=64 * 1024 * 1024),
+        compiler_params=pltpu.CompilerParams(vmem_limit_bytes=16 * 1024 * 1024),
         name="finish",
     )(shares)
     return recycled_c, recycled_u, coefficients[0]

time: 31 us -> 31.1 us (level)
  Pallas kernels: 29.5 us -> 28.1 us
  local copies, waits for them, and re-layouts: 0 us -> 1.37 us
    unnamed x0 -> x10, local copies, waits for them, and re-layouts: none -> 1.37 us
    pallas_call x1, Pallas kernels: 3.67 us -> 2.94 us  [per_device(): pl.pallas_call(functools.partial(finish, n_row * n_col * 2 * BLK), out_sh...]
    pallas_call x1, Pallas kernels: 25.8 us -> 25.2 us  [per_device(): pl.pallas_call(functools.partial(kernel, n_row, n_col, tile_rows, tile_co...]
where the time goes in v5:
time: 31.1 us; the launch traced here: 30.9 us
  Pallas kernels  28.1 us (90%)
  local copies, waits for them, and re-layouts  1.37 us (4%)
  between operations  1.37 us (4%)
    pallas_call x1, Pallas kernels, per_device(): pl.pallas_call(functools.partial(kernel, n_row, n_col, tile_rows, tile_co...  25.2 us
    pallas_call x1, Pallas kernels, per_device(): pl.pallas_call(functools.partial(finish, n_row * n_col * 2 * BLK), out_sh...  2.94 us
    unnamed x10, local copies, waits for them, and re-layouts  1.37 us

profile of v5, /device:TPU:0, one launch (start us, length us, event | category | flops | bytes accessed | tf_op | source)
XLA Modules:
  0.0 30.9 jit_solution(15314307766574648424)
XLA Ops:
  0.6 0.0 copy-start.3
  0.6 0.0 copy-start.2
  0.7 0.0 copy-start.1
  1.3 0.0 copy-done.3
  1.3 0.0 copy-done.2
  1.4 0.0 copy-done.1
  1.4 0.0 copy-start
  1.4 0.7 %copy-done = bf16[2,3072]{1,0:T(2,128)(2,1)S(1)} copy-done((bf16[2,3072]{1,0:T(2,128)(2,1)S(1)}, bf16[2,3072]{1,0:T(2,128)(2,1)}, u32[]{:S(2)}) %copy-start) | copy-done | bytes 12312
  2.1 0.0 copy-start.4
  2.1 0.7 %copy-done.4 = f32[128]{0:T(128)S(1)} copy-done((f32[128]{0:T(128)S(1)}, f32[128]{0:T(128)}, u32[]{:S(2)}) %copy-start.4) | copy-done | bytes 536
  2.7 25.2 %reduce.1.in_hbm = f32[112,128]{1,0:T(8,128)S(1)} custom-call(bf16[1,1,64,4096]{3,2,1,0:T(8,128)(2,1)} %tan_hbm.1, s32[1,1,64]{2,1,0:T(1,128)S(1)} %copy-done.1, s32[1,1,64]{2,1,0:T(1,128)S(1)} %copy-done.2, s32[1,1]{1,0:T(1,128)S(6)} %copy.10.count_hbm, bf16[2,3072]{1,0:T(2,128)(2,1)S(1)} %copy-done, s32[2]{0:T(128)S(1)} %copy-done.3, f32[128]{0:T(128)S(1)} %copy-done.4), custom_call_target="tpu_custom_call" | custom-call | tf_op jit(solution)/shard_map/reduce/pallas_call | solution.py:336
  27.9 2.9 %finish.1 = (bf16[2,3072]{1,0:T(2,128)(2,1)}, bf16[2,3072]{1,0:T(2,128)(2,1)}, f32[1,48]{1,0:T(1,128)}) custom-call(f32[112,128]{1,0:T(8,128)S(1)} %reduce.1.in_hbm), custom_call_target="tpu_custom_call" | custom-call | tf_op jit(solution)/shard_map/finish/pallas_call | solution.py:364
Async XLA Ops:
  0.6 0.7 %copy-start.3 = (s32[2]{0:T(128)S(1)}, s32[2]{0:T(128)}, u32[]{:S(2)}) copy-start(s32[2]{0:T(128)} %id_hbm.1) | copy-start | bytes 28
  0.6 0.7 %copy-start.2 = (s32[1,1,64]{2,1,0:T(1,128)S(1)}, s32[1,1,64]{2,1,0:T(1,128)}, u32[]{:S(2)}) copy-start(s32[1,1,64]{2,1,0:T(1,128)} %cols_hbm.1) | copy-start | bytes 772
  0.7 0.7 %copy-start.1 = (s32[1,1,64]{2,1,0:T(1,128)S(1)}, s32[1,1,64]{2,1,0:T(1,128)}, u32[]{:S(2)}) copy-start(s32[1,1,64]{2,1,0:T(1,128)} %rows_hbm.1) | copy-start | bytes 772
  1.4 0.7 %copy-start = (bf16[2,3072]{1,0:T(2,128)(2,1)S(1)}, bf16[2,3072]{1,0:T(2,128)(2,1)}, u32[]{:S(2)}) copy-start(bf16[2,3072]{1,0:T(2,128)(2,1)} %basis_hbm.1) | copy-start | bytes 36868
  2.1 0.7 %copy-start.4 = (f32[128]{0:T(128)S(1)}, f32[128]{0:T(128)}, u32[]{:S(2)}) copy-start(f32[128]{0:T(128)} %res_hbm.1) | copy-start | bytes 1540
